TPU v7x, 32 devices: a whole 2x2x4 slice. The times are simulated.
32 devices in a mesh: groups: 2 (over y), loop: 4 (over z), dp: 2 (over x), fsdp: 2 (over core).
Axes of the slice: x: 2, y: 2, z: 4, core: 2. Of those that a mesh axis runs over, the one named last changes fastest.
Arguments:
- activations: bfloat16 [768, 5120], P(('groups', 'dp')), parts along dimension 0, may hold values from -6 to 6
- cotangent: bfloat16 [768, 5120], P(('groups', 'dp')), parts along dimension 0, may hold values from -6 to 6
- weights_in: bfloat16 [864, 2, 5120], P(('loop', 'fsdp'), None, 'dp'), may hold values from -0.078125 to 0.078125
- weights_down: bfloat16 [864, 5120], P(('loop', 'fsdp'), 'dp'), may hold values from -0.21875 to 0.21875
- norm_gains: float32 [5120], replicated, may hold values from 0.1 to 1.9
Outputs:
- grad_in: float32 [1728, 2, 5120], P(('groups', 'loop', 'fsdp'), None, 'dp'), parts along dimension 0
- grad_down: float32 [1728, 5120], P(('groups', 'loop', 'fsdp'), 'dp'), parts along dimension 0
- grad_gains: float32 [10240], P('groups'), parts along dimension 0
- grad_act: bfloat16 [768, 5120], P(('groups', 'dp')), parts along dimension 0
There are 2 independent parts, one for each index of `groups`. A program takes and returns all parts, laid end to end along the dimension named above; an argument that names none is the same for every part. Nothing has to cross between parts.
All inputs are finite; a program needn't handle non-finite values.
Results may differ from a plain program's by a relative error of at most 0.0065.
Values may be sent and summed in bfloat16 or wider, within the bound.
A program may use at most 64 MiB of HBM per device.

v0:
```python
import jax
import jax.numpy as jnp
from jax import lax
from jax.sharding import PartitionSpec as P

EPSILON = 1e-05


def contract_rows(left, right):
    return lax.dot_general(
        left, right, (((0,), (0,)), ((), ())), preferred_element_type=jnp.float32
    )


def input_grad(d_normed, x_hat, inv_rms, cotangent, norm_gains):
    scaled = d_normed * norm_gains
    return (
        cotangent.astype(jnp.float32)
        + inv_rms * (scaled - x_hat * jnp.mean(scaled * x_hat, axis=-1, keepdims=True))
    ).astype(jnp.bfloat16)


def on_device(activations, cotangent, weights_in, weights_down, norm_gains):
    x_float = activations.astype(jnp.float32)
    inv_rms = lax.rsqrt(jnp.mean(x_float * x_float, axis=-1, keepdims=True) + EPSILON)
    x_hat = x_float * inv_rms
    normed = (x_hat * norm_gains).astype(jnp.bfloat16)
    full_in, full_down = (
        lax.all_gather(weights_in, "dp", axis=2, tiled=True),
        lax.all_gather(weights_down, "dp", axis=1, tiled=True),
    )
    gate_val = jnp.dot(normed, full_in[:, 0, :].T, preferred_element_type=jnp.float32)
    up_val = jnp.dot(normed, full_in[:, 1, :].T, preferred_element_type=jnp.float32)
    d_hidden = jnp.dot(cotangent, full_down.T, preferred_element_type=jnp.float32)
    sigma = jax.nn.sigmoid(gate_val)
    silu_val = gate_val * sigma
    hidden = (silu_val * up_val).astype(jnp.bfloat16)
    d_gate = (d_hidden * up_val * sigma * (1.0 + gate_val * (1.0 - sigma))).astype(jnp.bfloat16)
    d_up = (d_hidden * silu_val).astype(jnp.bfloat16)
    partial_normed = jnp.dot(
        d_gate, full_in[:, 0, :], preferred_element_type=jnp.float32
    ) + jnp.dot(d_up, full_in[:, 1, :], preferred_element_type=jnp.float32)
    d_normed = lax.psum(partial_normed, ("loop", "fsdp"))
    grad_gains = lax.psum(jnp.sum(d_normed * x_hat, axis=0), "dp")
    grad_act = input_grad(d_normed, x_hat, inv_rms, cotangent, norm_gains)
    term = jnp.stack(
        [
            contract_rows(d_gate, normed),
            contract_rows(d_up, normed),
            contract_rows(hidden, cotangent),
        ],
        axis=1,
    )
    term = lax.optimization_barrier(term.astype(jnp.bfloat16)).astype(jnp.float32)
    summed = lax.psum_scatter(
        term.astype(jnp.bfloat16), "dp", scatter_dimension=2, tiled=True
    ).astype(jnp.float32)
    return (summed[:, 0:2, :], summed[:, 2, :], grad_gains, grad_act)


def solution(mesh):
    return jax.shard_map(
        on_device,
        mesh=mesh,
        in_specs=(
            P(("groups", "dp"), None),
            P(("groups", "dp"), None),
            P(("loop", "fsdp"), None, "dp"),
            P(("loop", "fsdp"), "dp"),
            P(),
        ),
        out_specs=(
            P(("groups", "loop", "fsdp"), None, "dp"),
            P(("groups", "loop", "fsdp"), "dp"),
            P("groups"),
            P(("groups", "dp"), None),
        ),
        check_vma=False,
    )
```

profile of v0, /device:TPU:0, one launch (start us, length us, event | category | flops | bytes accessed | tf_op | source)
XLA Modules:
  0.0 233.7 jit_solution(13410951457832684418)
XLA Ops:
  7.2 0.0 all-gather.3.cloned.1.call-start
  7.2 0.7 all-gather.3.cloned.1.call-update
  7.9 0.0 copy-start
  7.9 0.0 all-gather.5.cloned.1.call-start
  8.0 2.5 %copy.10 = bf16[108,2,2560]{2,0,1:T(8,128)(2,1)} copy(bf16[108,2,2560]{2,1,0:T(2,128)(2,1)} %param.7) | data formatting | bytes 2211840 | tf_op args[2]
  10.4 0.0 all-gather.5.cloned.1.call-update
  10.5 0.0 copy-start.5
  10.5 0.0 all-reduce.2.cloned.1.call-start
  10.5 2.0 fusion.14
  12.6 22.1 %all-gather.3.cloned.1.call-done = bf16[108,5120]{1,0:T(8,128)(2,1)} async-done(((bf16[108,2560]{1,0:T(8,128)(2,1)}), bf16[108,5120]{1,0:T(8,128)(2,1)}) %all-gather.3.cloned.1.call-update) | async-done | bytes 1105936 | tf_op jit(solution)/shard_map/all_gather | solution.py:30
  34.7 0.0 copy-done
  34.7 1.9 fusion.25
  36.6 35.5 %all-gather.5.cloned.1.call-done = bf16[108,2,5120]{2,0,1:T(8,128)(2,1)} async-done(((bf16[108,2,2560]{2,0,1:T(8,128)(2,1)}), bf16[108,2,5120]{2,0,1:T(8,128)(2,1)}) %all-gather.5.cloned.1.call-update) | async-done | bytes 2211856 | tf_op jit(solution)/shard_map/all_gather | solution.py:29
  72.2 0.0 copy-done.5
  72.2 0.0 copy-start.1
  72.2 0.0 copy-start.4
  72.2 2.7 %fusion.15 = f32[192,108]{1,0:T(8,128)S(1)} fusion(bf16[108,2,5120]{2,0,1:T(8,128)(2,1)} %all-gather.5.cloned.1.call-done, bf16[192,5120]{1,0:T(8,128)(2,1)} %param.5, f32[5120]{0:T(1024)S(1)} %copy-done.5, f32[192]{0:T(256)S(1)} %add_rsqrt_fusion), kind=kOutput, calls=%fused_computation.25 | convolution fusion | flops 216268800 | bytes 3217152 | tf_op jit(solution)/shard_map/dot_general | solution.py:33
  74.9 0.0 copy-done.1
  74.9 0.4 copy-done.4
  75.3 0.8 multiply_convert_fusion.2
  76.1 0.7 fusion.16
  76.8 2.6 %convolution_add_fusion = f32[192,5120]{1,0:T(8,128)} fusion(f32[192,5120]{1,0:T(8,128)S(1)} %fusion.16, bf16[192,108]{1,0:T(8,128)(2,1)S(1)} %get-tuple-element.15, bf16[108,2,5120]{2,0,1:T(8,128)(2,1)S(1)} %copy-done.4), kind=kOutput, calls=%fused_computation | convolution fusion | flops 213319680 | bytes 9060352 | tf_op jit(solution)/shard_map/dot_general | solution.py:42
  79.4 0.0 all-reduce.2.cloned.1.call-update
  79.4 0.0 reduce-scatter.2.cloned.1.call-start
  79.5 0.0 copy-start.2
  79.5 0.5 fusion.2
  80.0 1.0 copy-done.2
  81.0 0.8 fusion
  81.8 0.8 fusion.1
  82.7 2.3 pad_maximum_fusion
  85.0 0.0 reduce-scatter.2.cloned.1.call-update
  85.0 86.2 %all-reduce.2.cloned.1.call-done = f32[192,5120]{1,0:T(8,128)} async-done(((f32[192,5120]{1,0:T(8,128)}), f32[192,5120]{1,0:T(8,128)}) %all-reduce.2.cloned.1.call-update) | async-done | bytes 3932176 | tf_op jit(solution)/shard_map/psum | solution.py:43
  171.1 3.9 %fusion.9 = (f32[192]{0:T(256)S(1)}, f32[5120]{0:T(1024)S(1)}) fusion(bf16[192,5120]{1,0:T(8,128)(2,1)} %param.5, f32[192,5120]{1,0:T(8,128)} %all-reduce.2.cloned.1.call-done, f32[5120]{0:T(1024)S(1)} %copy-done.5, f32[192]{0:T(256)S(1)} %add_rsqrt_fusion), kind=kLoop, calls=%fused_computation.15 | loop fusion | flops 6875968 | bytes 5940736 | tf_op jit(solution)/shard_map/reduce_sum | solution.py:19
  175.0 9.1 %psum.15 = f32[5120]{0:T(1024)} all-reduce(f32[5120]{0:T(1024)S(1)} %get-tuple-element.13), channel_id=1, replica_groups=mesh['groups'=2,'loop'=4,'dp'=2,'fsdp'=2] {'dp'}, use_global_device_ids=true, to_apply=%region_4.0 | all-reduce | flops 5120 | bytes 40960 | tf_op jit(solution)/shard_map/psum | solution.py:44
  184.1 5.3 %fusion.13 = bf16[192,5120]{1,0:T(8,128)(2,1)} fusion(bf16[192,5120]{1,0:T(8,128)(2,1)} %param.5, bf16[192,5120]{1,0:T(8,128)(2,1)S(1)} %copy-done, f32[192,5120]{1,0:T(8,128)} %all-reduce.2.cloned.1.call-done, f32[192]{0:T(256)S(1)} %broadcast_multiply_fusion, f32[5120]{0:T(1024)S(1)} %copy-done.5, f32[192]{0:T(256)S(1)} %add_rsqrt_fusion), kind=kLoop, calls=%fused_computation.19 | loop fusion | flops 8847360 | bytes 9852416 | tf_op jit(solution)/shard_map/convert_element_type | solution.py:20
  189.4 30.6 %reduce-scatter.2.cloned.1.call-done = bf16[108,3,2560]{2,0,1:T(8,128)(2,1)} async-done(((bf16[108,3,5120]{2,0,1:T(8,128)(2,1)}), bf16[108,3,2560]{2,0,1:T(8,128)(2,1)}) %reduce-scatter.2.cloned.1.call-update) | async-done | bytes 1658896 | tf_op jit(solution)/shard_map/reduce_scatter | solution.py:55
  220.0 1.9 convert_element_type.32
  221.9 0.0 copy-start.3
  221.9 1.1 slice_bitcast_fusion
  223.0 0.8 copy-done.3
  223.8 0.3 slice.20
  224.1 3.1 %copy.11 = f32[108,2,2560]{2,1,0:T(2,128)} copy(f32[108,2,2560]{2,0,1:T(8,128)S(1)} %slice.20) | data formatting | bytes 4423680
  (2 shorter events, 0.0 us)
Async XLA Ops:
  7.2 27.5 %all-gather.3.cloned.1.call-start = ((), (), s32[]{:S(2)}) async-start(), calls=%async_computation.1 | async-start | bytes 1720320 | tf_op jit(solution)/shard_map/all_gather | solution.py:30
  7.9 26.8 %copy-start = (bf16[192,5120]{1,0:T(8,128)(2,1)S(1)}, bf16[192,5120]{1,0:T(8,128)(2,1)}, u32[]{:S(2)}) copy-start(bf16[192,5120]{1,0:T(8,128)(2,1)} %param.6) | copy-start | bytes 5898244
  7.9 64.3 %all-gather.5.cloned.1.call-start = ((), (), s32[]{:S(2)}) async-start(), calls=%async_computation.2 | async-start | bytes 3440640 | tf_op jit(solution)/shard_map/all_gather | solution.py:29
  10.5 61.7 %copy-start.5 = (f32[5120]{0:T(1024)S(1)}, f32[5120]{0:T(1024)}, u32[]{:S(2)}) copy-start(f32[5120]{0:T(1024)} %param.9) | copy-start | bytes 61444
  10.5 160.7 %all-reduce.2.cloned.1.call-start = ((), (), s32[]{:S(2)}) async-start(), calls=%async_computation.4 | async-start | bytes 7864320 | tf_op jit(solution)/shard_map/psum | solution.py:43
  72.2 2.7 %copy-start.1 = (bf16[192,5120]{1,0:T(8,128)(2,1)S(1)}, bf16[192,5120]{1,0:T(8,128)(2,1)}, u32[]{:S(2)}) copy-start(bf16[192,5120]{1,0:T(8,128)(2,1)} %param.5) | copy-start | bytes 5898244
  72.2 3.2 %copy-start.4 = (bf16[108,2,5120]{2,0,1:T(8,128)(2,1)S(1)}, bf16[108,2,5120]{2,0,1:T(8,128)(2,1)}, u32[]{:S(2)}) copy-start(bf16[108,2,5120]{2,0,1:T(8,128)(2,1)} %all-gather.5.cloned.1.call-done) | copy-start | bytes 6635524
  79.4 140.6 %reduce-scatter.2.cloned.1.call-start = ((), (), s32[]{:S(2)}) async-start(), calls=%async_computation.3 | async-start | bytes 5160960 | tf_op jit(solution)/shard_map/reduce_scatter | solution.py:55
  79.5 1.5 copy-start.2
  221.9 1.9 copy-start.3
Sparse Core Ops, SparseCore 0:
  9.5 25.0 all-gather.2
  36.8 35.3 all-gather.4
  79.5 91.5 all-reduce.1
  173.2 46.7 reduce-scatter.1
where the time goes:
time: 234 us
  waiting for transfers between devices  175 us (75%)
  other arithmetic  15.4 us (7%)
  between operations  13.9 us (6%)
  matrix products  10.8 us (5%)
  local copies, waits for them, and re-layouts  9.14 us (4%)
  blocking collectives  9.05 us (4%)
    psum x1, waiting for transfers between devices, on_device(): d_normed = lax.psum(partial_normed, ('loop', 'fsdp'))  86.2 us
    all_gather x1, waiting for transfers between devices, on_device(): lax.all_gather(weights_in, 'dp', axis=2, tiled=True)  35.5 us
    reduce_scatter x1, waiting for transfers between devices, on_device(): lax.psum_scatter(term.astype(jnp.bfloat16), 'dp', scatter_dimension=2, ti...  30.6 us
    all_gather x1, waiting for transfers between devices, on_device(): lax.all_gather(weights_down, 'dp', axis=1, tiled=True)  22.1 us
    psum x1, blocking collectives, on_device(): grad_gains = lax.psum(jnp.sum(d_normed * x_hat, axis=0), 'dp')  9.05 us
    unnamed x14, local copies, waits for them, and re-layouts  7.8 us
    convert_element_type x1, other arithmetic, input_grad(): return (cotangent.astype(jnp.float32) + inv_rms * (scaled - x_hat * jnp.m...  5.3 us
  transfers between devices with their start and end apart: 4, of which 4 were waited for; matrix products, arithmetic and copies ran while one was open for 9% of the time, Pallas kernels for 0%

commit v1 on v0

--- a/solution.py
+++ b/solution.py
@@ -1,6 +1,10 @@
+import functools
+
 import jax
 import jax.numpy as jnp
 from jax import lax
+from jax.experimental import pallas as pl
+from jax.experimental.pallas import tpu as pltpu
 from jax.sharding import PartitionSpec as P
 
 EPSILON = 1e-05
@@ -58,9 +62,277 @@
     return (summed[:, 0:2, :], summed[:, 2, :], grad_gains, grad_act)
 
 
+HP = 128
+
+
+def dot_t(left, right):
+    return lax.dot_general(
+        left, right, (((1,), (1,)), ((), ())), preferred_element_type=jnp.float32
+    )
+
+
+def fused_kernel(
+    L, act, cot, wgu, wd, gains,
+    g_gate, g_up, g_down, g_gains, out,
+    normed, xhat, inv_s, cotf, tok_x, part, part_x, dgu, hid,
+    dn, p_buf, r_buf, qf, q_buf, rz, t_buf, t_x, fin, gsum, gx, gc, gz,
+    s_x, r_x, s_c, r_c, s_p, r_p, s_d, r_d, s_z, r_z, s_t, r_t,
+    s_ag, r_ag, s_fw, r_fw, s_g, r_g, s_gz, r_gz,
+):
+    tok, width = act.shape
+    half = width // 2
+    hb = tok // 2
+    ch = tok // (2 * L)
+    l, d, f = lax.axis_index("loop"), lax.axis_index("dp"), lax.axis_index("fsdp")
+    mine = pl.ds(pl.multiple_of(d * half, 128), half)
+    theirs = pl.ds(pl.multiple_of((1 - d) * half, 128), half)
+    x_dev, c_dev = {"dp": 1 - d}, {"fsdp": 1 - f}
+    to = [lax.rem(l + k, L) for k in range(L)]
+    frm = [lax.rem(l - k + L, L) for k in range(L)]
+
+    def rc(src, dst, ss, rs, dev):
+        return pltpu.make_async_remote_copy(
+            src_ref=src, dst_ref=dst, send_sem=ss, recv_sem=rs,
+            device_id=dev, device_id_type=pl.DeviceIdType.MESH,
+        )
+
+    barrier = pltpu.get_barrier_semaphore()
+    for dev in [x_dev, c_dev] + [{"loop": to[k]} for k in range(1, L)]:
+        pl.semaphore_signal(barrier, inc=1, device_id=dev, device_id_type=pl.DeviceIdType.MESH)
+    pl.semaphore_wait(barrier, L + 1)
+
+    my_rows = pl.ds(pl.multiple_of(f * hb, 16), hb)
+    x_cot = rc(cot.at[my_rows, theirs], tok_x.at[1, my_rows], s_x.at[1], r_x.at[1], x_dev)
+    x_cot.start()
+
+    def norm_rows(start):
+        def body(i, carry):
+            rows = pl.ds(pl.multiple_of(start + i * 16, 16), 16)
+            x = act[rows, :].astype(jnp.float32)
+            inv = lax.rsqrt(jnp.mean(x * x, axis=-1, keepdims=True) + EPSILON)
+            xh = x * inv
+            xhat[rows, :] = xh
+            inv_s[rows, :] = jnp.broadcast_to(inv, (16, 128))
+            normed[rows, :] = (xh * gains[...]).astype(jnp.bfloat16)
+            return carry
+
+        lax.fori_loop(0, hb // 16, body, 0)
+
+    norm_rows(f * hb)
+    x_nrm = rc(normed.at[my_rows, theirs], tok_x.at[0, my_rows], s_x.at[0], r_x.at[0], x_dev)
+    x_nrm.start()
+    norm_rows((1 - f) * hb)
+
+    part[0, 2] = dot_t(cot[:, mine], wd[...])
+    gu = dot_t(normed[:, mine], wgu[...])
+    part[0, 0] = gu[:, :HP]
+    part[0, 1] = gu[:, HP:]
+    part_x[0] = part[0].astype(jnp.bfloat16)
+    p_own = rc(part_x.at[0], part_x.at[3], s_p.at[0], r_p.at[0], x_dev)
+    p_own.start()
+
+    def cot_body(i, carry):
+        rows = pl.ds(pl.multiple_of(i * 16, 16), 16)
+        cotf[rows, :] = cot[rows, :].astype(jnp.float32)
+        return carry
+
+    lax.fori_loop(0, tok // 16, cot_body, 0)
+
+    x_cot.wait()
+    c_cot = rc(tok_x.at[1, my_rows], tok_x.at[1, my_rows], s_c.at[1], r_c.at[1], c_dev)
+    c_cot.start()
+    x_nrm.wait()
+    c_nrm = rc(tok_x.at[0, my_rows], tok_x.at[0, my_rows], s_c.at[0], r_c.at[0], c_dev)
+    c_nrm.start()
+    c_cot.wait()
+    part[1, 2] = dot_t(tok_x[1], wd[...])
+    c_nrm.wait()
+    gu = dot_t(tok_x[0], wgu[...])
+    part[1, 0] = gu[:, :HP]
+    part[1, 1] = gu[:, HP:]
+    part_x[1] = part[1].astype(jnp.bfloat16)
+    p_oth = rc(part_x.at[1], part_x.at[2], s_p.at[1], r_p.at[1], x_dev)
+    p_oth.start()
+
+    def hidden_grads(t):
+        gate = part[t, 0] + part_x[2 + t, 0].astype(jnp.float32)
+        up = part[t, 1] + part_x[2 + t, 1].astype(jnp.float32)
+        dh = part[t, 2] + part_x[2 + t, 2].astype(jnp.float32)
+        sig = jax.nn.sigmoid(gate)
+        silu = gate * sig
+        hid[t] = (silu * up).astype(jnp.bfloat16)
+        dgu[t, :, :HP] = (dh * up * sig * (1.0 + gate * (1.0 - sig))).astype(jnp.bfloat16)
+        dgu[t, :, HP:] = (dh * silu).astype(jnp.bfloat16)
+
+        def body(i, carry):
+            cols = pl.ds(pl.multiple_of(i * 512, 128), 512)
+            dn[t, :, cols] = jnp.dot(
+                dgu[t], wgu[:, cols], preferred_element_type=jnp.float32
+            )
+            return carry
+
+        lax.fori_loop(0, half // 512, body, 0)
+        for j in range(L):
+            rows = pl.ds(pl.multiple_of((2 * j + 1 - f) * ch, 8), ch)
+            p_buf[t, j] = dn[t, rows, :].astype(jnp.bfloat16)
+        copy = rc(p_buf.at[t], r_buf.at[t], s_d.at[t], r_d.at[t], c_dev)
+        copy.start()
+        return copy
+
+    p_own.wait()
+    d1 = hidden_grads(1)
+    p_oth.wait()
+    d0 = hidden_grads(0)
+
+    zc = {}
+    for t, dd in ((1, d1), (0, d0)):
+        dd.wait()
+        for k in (L // 2, *[k for k in range(1, L) if k != L // 2], 0):
+            rows = pl.ds(pl.multiple_of((2 * to[k] + f) * ch, 8), ch)
+            val = dn[t, rows, :] + r_buf[t, to[k]].astype(jnp.float32)
+            if k == 0:
+                qf[t] = val
+            else:
+                q_buf[k, t] = val.astype(jnp.bfloat16)
+                zc[k, t] = rc(q_buf.at[k, t], rz.at[k, t], s_z.at[k, t], r_z.at[k, t], {"loop": to[k]})
+                zc[k, t].start()
+
+    def wg_body(i, carry):
+        cols = pl.ds(pl.multiple_of(i * 256, 128), 256)
+        own = pl.ds(pl.multiple_of(d * half + i * 256, 128), 256)
+        gu = contract_rows(dgu[0], normed[:, own]) + contract_rows(dgu[1], tok_x[0, :, cols])
+        rows = g_gate.shape[0]
+        g_gate[:, cols] = gu[:rows]
+        g_up[:, cols] = gu[HP : HP + rows]
+        down = contract_rows(hid[0], cot[:, own]) + contract_rows(hid[1], tok_x[1, :, cols])
+        g_down[:, cols] = down[:rows]
+        return carry
+
+    lax.fori_loop(0, half // 256, wg_body, 0)
+
+    def total(t):
+        for k in range(1, L):
+            zc[k, t].wait()
+        val = qf[t]
+        for k in range(1, L):
+            val = val + rz[k, t].astype(jnp.float32)
+        return val
+
+    t_buf[...] = total(1).astype(jnp.bfloat16)
+    tc = rc(t_buf, t_x, s_t.at[0], r_t.at[0], x_dev)
+    tc.start()
+    fin[:, mine] = total(0)
+    tc.wait()
+    fin[:, theirs] = t_x[...].astype(jnp.float32)
+
+    rows = pl.ds(pl.multiple_of((2 * l + f) * ch, 8), ch)
+    dnf = fin[...]
+    xh = xhat[rows, :]
+    scaled = dnf * gains[...]
+    mean = jnp.mean(scaled * xh, axis=-1, keepdims=True)
+    res = cotf[rows, :] + inv_s[rows, :1] * (scaled - xh * mean)
+    slot = 2 * l + f
+    out[slot] = res.astype(jnp.bfloat16)
+    ag = {}
+    for k in (L // 2, *[k for k in range(1, L) if k != L // 2]):
+        ag[k] = rc(out.at[slot], out.at[slot], s_ag.at[k], r_ag.at[k], {"loop": to[k]})
+        ag[k].start()
+    fw = {0: rc(out.at[slot], out.at[slot], s_fw.at[0], r_fw.at[0], c_dev)}
+    fw[0].start()
+
+    gsums = jnp.sum(dnf * xh, axis=0, keepdims=True)
+    for i in range(8):
+        gsum[0, i : i + 1, :] = gsums[:, i * (width // 8) : (i + 1) * (width // 8)]
+    ga = rc(gsum.at[0], gx, s_g.at[0], r_g.at[0], x_dev)
+    ga.start()
+    ga.wait()
+    gsum[1] = gsum[0] + gx[...]
+    gb = rc(gsum.at[1], gc, s_g.at[1], r_g.at[1], c_dev)
+    gb.start()
+    gb.wait()
+    gz[l] = gsum[1] + gc[...]
+    gcopies = []
+    for k in range(1, L):
+        gcopies.append(rc(gz.at[l], gz.at[l], s_gz.at[k], r_gz.at[k], {"loop": to[k]}))
+        gcopies[-1].start()
+
+    for k in range(1, L):
+        ag[k].wait()
+        got = 2 * frm[k] + f
+        fw[k] = rc(out.at[got], out.at[got], s_fw.at[k], r_fw.at[k], c_dev)
+        fw[k].start()
+    for copy in gcopies:
+        copy.wait()
+    acc = gz[0]
+    for j in range(1, L):
+        acc = acc + gz[j]
+    g_gains[...] = acc
+    for k in range(L):
+        fw[k].wait()
+
+
+def on_device_fused(L, activations, cotangent, weights_in, weights_down, norm_gains):
+    tok, width = activations.shape
+    hidden, half = weights_down.shape
+    ch = tok // (2 * L)
+    pad = ((0, HP - hidden), (0, 0))
+    wgu = jnp.concatenate([jnp.pad(weights_in[:, 0], pad), jnp.pad(weights_in[:, 1], pad)], axis=0)
+    wd = jnp.pad(weights_down, pad)
+    bf, f32 = jnp.bfloat16, jnp.float32
+    vm, sem = pltpu.VMEM, pltpu.SemaphoreType.DMA
+    spec = pl.BlockSpec(memory_space=pltpu.VMEM)
+    shape = jax.ShapeDtypeStruct
+    g_gate, g_up, g_down, g_gains, out = pl.pallas_call(
+        functools.partial(fused_kernel, L),
+        out_shape=(
+            shape((hidden, half), f32), shape((hidden, half), f32), shape((hidden, half), f32),
+            shape((8, width // 8), f32), shape((2 * L, ch, width), bf),
+        ),
+        in_specs=[spec] * 5,
+        out_specs=(spec,) * 5,
+        scratch_shapes=[
+            vm((tok, width), bf), vm((tok, width), f32), vm((tok, 128), f32), vm((tok, width), f32),
+            vm((2, tok, half), bf),
+            vm((2, 3, tok, HP), f32), vm((4, 3, tok, HP), bf),
+            vm((2, tok, 2 * HP), bf), vm((2, tok, HP), bf),
+            vm((2, tok, half), f32), vm((2, L, ch, half), bf), vm((2, L, ch, half), bf),
+            vm((2, ch, half), f32), vm((L, 2, ch, half), bf), vm((L, 2, ch, half), bf),
+            vm((ch, half), bf), vm((ch, half), bf), vm((ch, width), f32),
+            vm((2, 8, width // 8), f32), vm((8, width // 8), f32), vm((8, width // 8), f32),
+            vm((L, 8, width // 8), f32),
+            sem((2,)), sem((2,)), sem((2,)), sem((2,)), sem((2,)), sem((2,)), sem((2,)), sem((2,)),
+            sem((L, 2)), sem((L, 2)), sem((1,)), sem((1,)),
+            sem((L,)), sem((L,)), sem((L,)), sem((L,)), sem((2,)), sem((2,)), sem((L,)), sem((L,)),
+        ],
+        compiler_params=pltpu.CompilerParams(
+            collective_id=0, has_side_effects=True, vmem_limit_bytes=58 * 2**20
+        ),
+    )(activations, cotangent, wgu, wd, norm_gains[None, :])
+    return (
+        jnp.stack([g_gate, g_up], axis=1), g_down, g_gains.reshape(width), out.reshape(tok, width),
+    )
+
+
+def body_for(mesh, args_tok, hidden):
+    L = mesh.shape["loop"]
+    fits = hidden <= HP and mesh.shape["dp"] == 2 and mesh.shape["fsdp"] == 2 and args_tok % (16 * L) == 0
+    return functools.partial(on_device_fused, L) if fits and L > 1 else on_device
+
+
 def solution(mesh):
+    def run(activations, cotangent, weights_in, weights_down, norm_gains):
+        tok = activations.shape[0] // (mesh.shape["groups"] * mesh.shape["dp"])
+        hidden = weights_down.shape[0] // (mesh.shape["loop"] * mesh.shape["fsdp"])
+        return mapped(mesh, body_for(mesh, tok, hidden))(
+            activations, cotangent, weights_in, weights_down, norm_gains
+        )
+
+    return run
+
+
+def mapped(mesh, body):
     return jax.shard_map(
-        on_device,
+        body,
         mesh=mesh,
         in_specs=(
             P(("groups", "dp"), None),

time: 234 us -> 102 us (0.44)
  waiting for transfers between devices: 175 us -> 0 us
  Pallas kernels: 0 us -> 88.2 us
  between operations: 13.9 us -> 0.69 us
  other arithmetic: 15.4 us -> 2.91 us
  matrix products: 10.8 us -> 0 us
  blocking collectives: 9.05 us -> 0 us
    pallas_call x0 -> x1, Pallas kernels: none -> 88.2 us  [on_device_fused(): pl.pallas_call(functools.partial(fused_kernel, L), out_shape=(shape((hidd...]
    psum x1 -> x0, waiting for transfers between devices: 86.2 us -> none  [on_device(): d_normed = lax.psum(partial_normed, ('loop', 'fsdp'))]
    all_gather x2 -> x0, waiting for transfers between devices: 57.7 us -> none  [the longest x1 35.5 us: on_device(): lax.all_gather(weights_in, 'dp', axis=2, tiled=True)]
    reduce_scatter x1 -> x0, waiting for transfers between devices: 30.6 us -> none  [on_device(): lax.psum_scatter(term.astype(jnp.bfloat16), 'dp', scatter_dimension=2, ti...]
    dot_general x8 -> x0, matrix products: 10.8 us -> none  [the longest x1 2.72 us: on_device(): jnp.dot(normed, full_in[:, 1, :].T, preferred_element_type=jnp.float32)]
    psum x1 -> x0, blocking collectives: 9.05 us -> none  [on_device(): grad_gains = lax.psum(jnp.sum(d_normed * x_hat, axis=0), 'dp')]
    convert_element_type x2 -> x0, other arithmetic: 7.17 us -> none  [the longest x1 5.3 us: input_grad(): return (cotangent.astype(jnp.float32) + inv_rms * (scaled - x_hat * jnp.m...]
    reduce_sum x2 -> x0, other arithmetic: 5.93 us -> none  [the longest x1 3.91 us: input_grad(): jnp.mean(scaled * x_hat, axis=-1, keepdims=True)]
  transfers between devices with their start and end apart: 4 -> 0, of which waited for: 4 -> 0; matrix products, arithmetic and copies ran while one was open for 9% -> 0% of each run, Pallas kernels for 0% -> 0%
where the time goes in v1:
time: 102 us; the launch traced here: 101 us
  Pallas kernels  88.2 us (86%)
  local copies, waits for them, and re-layouts  9.7 us (10%)
  other arithmetic  2.91 us (3%)
    pallas_call x1, Pallas kernels, on_device_fused(): pl.pallas_call(functools.partial(fused_kernel, L), out_shape=(shape((hidd...  88.2 us
    unnamed x11, local copies, waits for them, and re-layouts  5.35 us

profile of v1, /device:TPU:0, one launch (start us, length us, event | category | flops | bytes accessed | tf_op | source)
XLA Modules:
  0.0 101.5 jit_solution(3708290355040687327)
XLA Ops:
  0.6 0.0 copy-start
  0.6 2.0 %pad.12.wd = bf16[128,2560]{1,0:T(8,128)(2,1)} pad(bf16[108,2560]{1,0:T(8,128)(2,1)} %param.8, bf16[]{:T(256)} %constant.2.clone.1), padding=0_20x0_0 | pad | bytes 1208322 | tf_op jit(solution)/shard_map/jit(_pad)/pad | solution.py:280
  2.7 0.0 copy-done
  2.7 1.6 %fusion.3 = (bf16[108,1,2560]{2,1,0:T(2,128)(2,1)S(1)}, bf16[108,1,2560]{2,1,0:T(2,128)(2,1)S(1)}) fusion(bf16[108,2,2560]{2,1,0:T(2,128)(2,1)S(1)} %copy-done), kind=kLoop, calls=%fused_computation.8 | loop fusion | bytes 2211840 | tf_op jit(solution)/shard_map/slice | solution.py:279
  4.2 0.2 copy_bitcast_fusion
  4.4 1.1 %fusion.2.wgu = bf16[256,2560]{1,0:T(8,128)(2,1)} fusion(bf16[108,2560]{1,0:T(8,128)(2,1)S(1)} %get-tuple-element.20, bf16[108,2560]{1,0:T(8,128)(2,1)S(1)} %get-tuple-element.21), kind=kLoop, calls=%fused_computation.5 | loop fusion | flops 5242880 | bytes 2416640 | tf_op jit(solution)/shard_map/concatenate | solution.py:279
  5.5 88.2 %shard_map.84 = (f32[108,2560]{1,0:T(8,128)}, f32[108,2560]{1,0:T(8,128)}, f32[108,2560]{1,0:T(8,128)}, f32[8,640]{1,0:T(8,128)}, bf16[8,24,5120]{2,1,0:T(8,128)(2,1)}) custom-call(bf16[192,5120]{1,0:T(8,128)(2,1)} %act.1, bf16[192,5120]{1,0:T(8,128)(2,1)} %cot.1, bf16[256,2560]{1,0:T(8,128)(2,1)} %fusion.2.wgu, bf16[128,2560]{1,0:T(8,128)(2,1)} %pad.12.wd, ...), custom_call_target="tpu_custom_call" | custom-call | tf_op jit(solution)/shard_map/pallas_call | solution.py:285
  93.7 1.8 %pad_maximum_fusion = f32[108,2,2560]{2,0,1:T(8,128)S(1)} fusion(f32[108,1,2560]{2,0,1:T(8,128)} %bitcast.10, f32[108,1,2560]{2,0,1:T(8,128)} %bitcast.9), kind=kLoop, calls=%fused_computation.4 | loop fusion | flops 552960 | bytes 4423680 | tf_op jit(solution)/shard_map/stack | solution.py:312
  95.5 0.0 copy-start.3
  95.5 0.0 copy-start.2
  95.5 3.1 %copy.11 = f32[108,2,2560]{2,1,0:T(2,128)} copy(f32[108,2,2560]{2,0,1:T(8,128)S(1)} %pad_maximum_fusion) | data formatting | bytes 4423680
  98.6 0.0 copy-done.3
  98.6 0.0 copy-start.1
  98.6 0.6 reshape.14
  99.2 0.0 copy-done.2
  99.2 1.0 copy.18
  100.2 0.0 copy-done.1
  100.2 1.3 %copy.19 = bf16[192,5120]{1,0:T(8,128)(2,1)} copy(bf16[192,5120]{1,0:T(8,128)(2,1)S(1)} %bitcast.8) | data formatting | bytes 3932160
Async XLA Ops:
  0.6 2.0 %copy-start = (bf16[108,2,2560]{2,1,0:T(2,128)(2,1)S(1)}, bf16[108,2,2560]{2,1,0:T(2,128)(2,1)}, u32[]{:S(2)}) copy-start(bf16[108,2,2560]{2,1,0:T(2,128)(2,1)} %param.7) | copy-start | bytes 3317764
  95.5 3.1 %copy-start.3 = (f32[8,640]{1,0:T(8,128)S(1)}, f32[8,640]{1,0:T(8,128)}, u32[]{:S(2)}) copy-start(f32[8,640]{1,0:T(8,128)} %get-tuple-element.12) | copy-start | bytes 61444
  95.5 3.7 %copy-start.2 = (f32[108,2560]{1,0:T(8,128)S(1)}, f32[108,2560]{1,0:T(8,128)}, u32[]{:S(2)}) copy-start(f32[108,2560]{1,0:T(8,128)} %get-tuple-element.27) | copy-start | bytes 3317764
  98.6 1.6 %copy-start.1 = (bf16[8,24,5120]{2,1,0:T(8,128)(2,1)S(1)}, bf16[8,24,5120]{2,1,0:T(8,128)(2,1)}, u32[]{:S(2)}) copy-start(bf16[8,24,5120]{2,1,0:T(8,128)(2,1)} %get-tuple-element.13) | copy-start | bytes 5898244

commit v2 on v1

--- a/solution.py
+++ b/solution.py
@@ -72,9 +72,9 @@
 
 
 def fused_kernel(
-    L, act, cot, wgu, wd, gains,
+    L, act, cot, w_in, w_down, gains,
     g_gate, g_up, g_down, g_gains, out,
-    normed, xhat, inv_s, cotf, tok_x, part, part_x, dgu, hid,
+    wgu, wd, normed, xhat, inv_s, cotf, tok_x, part, part_x, dgu, hid,
     dn, p_buf, r_buf, qf, q_buf, rz, t_buf, t_x, fin, gsum, gx, gc, gz,
     s_x, r_x, s_c, r_c, s_p, r_p, s_d, r_d, s_z, r_z, s_t, r_t,
     s_ag, r_ag, s_fw, r_fw, s_g, r_g, s_gz, r_gz,
@@ -88,7 +88,6 @@
     theirs = pl.ds(pl.multiple_of((1 - d) * half, 128), half)
     x_dev, c_dev = {"dp": 1 - d}, {"fsdp": 1 - f}
     to = [lax.rem(l + k, L) for k in range(L)]
-    frm = [lax.rem(l - k + L, L) for k in range(L)]
 
     def rc(src, dst, ss, rs, dev):
         return pltpu.make_async_remote_copy(
@@ -122,6 +121,12 @@
     x_nrm = rc(normed.at[my_rows, theirs], tok_x.at[0, my_rows], s_x.at[0], r_x.at[0], x_dev)
     x_nrm.start()
     norm_rows((1 - f) * hb)
+    hidden = w_down.shape[0]
+    low = hidden // 16 * 16
+    for base, dst, src in ((0, wgu, w_in.at[0]), (HP, wgu, w_in.at[1]), (0, wd, w_down)):
+        if low < HP:
+            dst[base + low : base + HP] = jnp.zeros((HP - low, half), jnp.bfloat16)
+        dst[base : base + hidden] = src[...]
 
     part[0, 2] = dot_t(cot[:, mine], wd[...])
     gu = dot_t(normed[:, mine], wgu[...])
@@ -180,43 +185,78 @@
         return copy
 
     p_own.wait()
+    steps = [(w, t, k) for k in range(L - 1) for w in (0, 1) for t in (1, 0)]
+    ahead = [l + 1, l - 1]
+    has_next, has_prev = [l < L - 1, l > 0], [l > 0, l < L - 1]
+
+    def target(w, k):
+        return L - 1 - k if w == 0 else k
+
+    def beyond(w, j):
+        return l < j if w == 0 else l > j
+
+    def own(t, j):
+        rows = pl.ds(pl.multiple_of((2 * j + f) * ch, 8), ch)
+        return dn[t, rows, :] + r_buf[t, j].astype(jnp.float32)
+
+    def line(w, t, k):
+        return rc(
+            q_buf.at[w, k, t], rz.at[w, k, t], s_z.at[w, k, t], r_z.at[w, k, t], {"loop": ahead[w]}
+        )
+
+    def first_sends(t):
+        for k in range(L - 1):
+            for w in (0, 1):
+
+                @pl.when(jnp.logical_not(has_prev[w]))
+                def _():
+                    q_buf[w, k, t] = own(t, target(w, k)).astype(jnp.bfloat16)
+                    line(w, t, k).start()
+
+    def pass_on(w, t, k):
+        @pl.when(jnp.logical_and(has_prev[w], beyond(w, target(w, k))))
+        def _():
+            line(w, t, k).wait_recv()
+            val = own(t, target(w, k)) + rz[w, k, t].astype(jnp.float32)
+            q_buf[w, k, t] = val.astype(jnp.bfloat16)
+            line(w, t, k).start()
+
     d1 = hidden_grads(1)
+    d1.wait()
+    first_sends(1)
     p_oth.wait()
     d0 = hidden_grads(0)
-
-    zc = {}
-    for t, dd in ((1, d1), (0, d0)):
-        dd.wait()
-        for k in (L // 2, *[k for k in range(1, L) if k != L // 2], 0):
-            rows = pl.ds(pl.multiple_of((2 * to[k] + f) * ch, 8), ch)
-            val = dn[t, rows, :] + r_buf[t, to[k]].astype(jnp.float32)
-            if k == 0:
-                qf[t] = val
-            else:
-                q_buf[k, t] = val.astype(jnp.bfloat16)
-                zc[k, t] = rc(q_buf.at[k, t], rz.at[k, t], s_z.at[k, t], r_z.at[k, t], {"loop": to[k]})
-                zc[k, t].start()
+    d0.wait()
+    first_sends(0)
 
     def wg_body(i, carry):
         cols = pl.ds(pl.multiple_of(i * 256, 128), 256)
-        own = pl.ds(pl.multiple_of(d * half + i * 256, 128), 256)
-        gu = contract_rows(dgu[0], normed[:, own]) + contract_rows(dgu[1], tok_x[0, :, cols])
-        rows = g_gate.shape[0]
-        g_gate[:, cols] = gu[:rows]
-        g_up[:, cols] = gu[HP : HP + rows]
-        down = contract_rows(hid[0], cot[:, own]) + contract_rows(hid[1], tok_x[1, :, cols])
-        g_down[:, cols] = down[:rows]
+        own_cols = pl.ds(pl.multiple_of(d * half + i * 256, 128), 256)
+        gu = contract_rows(dgu[0], normed[:, own_cols]) + contract_rows(dgu[1], tok_x[0, :, cols])
+        g_gate[:, cols] = gu[:hidden]
+        g_up[:, cols] = gu[HP : HP + hidden]
+        down = contract_rows(hid[0], cot[:, own_cols]) + contract_rows(hid[1], tok_x[1, :, cols])
+        g_down[:, cols] = down[:hidden]
         return carry
 
-    lax.fori_loop(0, half // 256, wg_body, 0)
+    tiles = half // 256
+    for k in range(L - 1):
+        for w in (0, 1):
+            pass_on(w, 1, k)
+        for w in (0, 1):
+            pass_on(w, 0, k)
+        lax.fori_loop(tiles * k // (L - 1), tiles * (k + 1) // (L - 1), wg_body, 0)
 
     def total(t):
-        for k in range(1, L):
-            zc[k, t].wait()
-        val = qf[t]
-        for k in range(1, L):
-            val = val + rz[k, t].astype(jnp.float32)
-        return val
+        qf[t] = own(t, l)
+        for w, at in ((0, L - 1 - l), (1, l)):
+
+            @pl.when(has_prev[w])
+            def _():
+                line(w, t, at).wait_recv()
+                qf[t] = qf[t] + rz[w, at, t].astype(jnp.float32)
+
+        return qf[t]
 
     t_buf[...] = total(1).astype(jnp.bfloat16)
     tc = rc(t_buf, t_x, s_t.at[0], r_t.at[0], x_dev)
@@ -233,12 +273,29 @@
     res = cotf[rows, :] + inv_s[rows, :1] * (scaled - xh * mean)
     slot = 2 * l + f
     out[slot] = res.astype(jnp.bfloat16)
-    ag = {}
-    for k in (L // 2, *[k for k in range(1, L) if k != L // 2]):
-        ag[k] = rc(out.at[slot], out.at[slot], s_ag.at[k], r_ag.at[k], {"loop": to[k]})
-        ag[k].start()
-    fw = {0: rc(out.at[slot], out.at[slot], s_fw.at[0], r_fw.at[0], c_dev)}
-    fw[0].start()
+
+    def chunk(w, k):
+        return out.at[2 * (l - k if w == 0 else l + k) + f]
+
+    def has(w, k):
+        return l - k >= 0 if w == 0 else l + k < L
+
+    def gather(w, k):
+        return rc(chunk(w, k), chunk(w, k), s_ag.at[w, k], r_ag.at[w, k], {"loop": ahead[w]})
+
+    def came(w, k):
+        return rc(chunk(w, k), chunk(w, k), s_ag.at[w, k - 1], r_ag.at[w, k - 1], {"loop": ahead[w]})
+
+    def across(w, k):
+        return rc(chunk(w, k), chunk(w, k), s_fw.at[w, k], r_fw.at[w, k], c_dev)
+
+    for w in (0, 1):
+
+        @pl.when(has_next[w])
+        def _():
+            gather(w, 0).start()
+
+    across(0, 0).start()
 
     gsums = jnp.sum(dnf * xh, axis=0, keepdims=True)
     for i in range(8):
@@ -257,27 +314,50 @@
         gcopies[-1].start()
 
     for k in range(1, L):
-        ag[k].wait()
-        got = 2 * frm[k] + f
-        fw[k] = rc(out.at[got], out.at[got], s_fw.at[k], r_fw.at[k], c_dev)
-        fw[k].start()
+        for w in (0, 1):
+
+            @pl.when(has(w, k))
+            def _():
+                came(w, k).wait_recv()
+                if k < L - 1:
+
+                    @pl.when(has_next[w])
+                    def _():
+                        gather(w, k).start()
+
+                across(w, k).start()
+
     for copy in gcopies:
         copy.wait()
     acc = gz[0]
     for j in range(1, L):
         acc = acc + gz[j]
     g_gains[...] = acc
-    for k in range(L):
-        fw[k].wait()
+    across(0, 0).wait()
+    for w in (0, 1):
+        for k in range(1, L):
+
+            @pl.when(has(w, k))
+            def _():
+                across(w, k).wait()
+
+        for k in range(L - 1):
+
+            @pl.when(jnp.logical_and(has(w, k), has_next[w]))
+            def _():
+                gather(w, k).wait_send()
+
+    for w, t, k in steps:
+
+        @pl.when(beyond(w, target(w, k)))
+        def _():
+            line(w, t, k).wait_send()
 
 
 def on_device_fused(L, activations, cotangent, weights_in, weights_down, norm_gains):
     tok, width = activations.shape
     hidden, half = weights_down.shape
     ch = tok // (2 * L)
-    pad = ((0, HP - hidden), (0, 0))
-    wgu = jnp.concatenate([jnp.pad(weights_in[:, 0], pad), jnp.pad(weights_in[:, 1], pad)], axis=0)
-    wd = jnp.pad(weights_down, pad)
     bf, f32 = jnp.bfloat16, jnp.float32
     vm, sem = pltpu.VMEM, pltpu.SemaphoreType.DMA
     spec = pl.BlockSpec(memory_space=pltpu.VMEM)
@@ -291,23 +371,24 @@
         in_specs=[spec] * 5,
         out_specs=(spec,) * 5,
         scratch_shapes=[
+            vm((2 * HP, half), bf), vm((HP, half), bf),
             vm((tok, width), bf), vm((tok, width), f32), vm((tok, 128), f32), vm((tok, width), f32),
             vm((2, tok, half), bf),
             vm((2, 3, tok, HP), f32), vm((4, 3, tok, HP), bf),
             vm((2, tok, 2 * HP), bf), vm((2, tok, HP), bf),
             vm((2, tok, half), f32), vm((2, L, ch, half), bf), vm((2, L, ch, half), bf),
-            vm((2, ch, half), f32), vm((L, 2, ch, half), bf), vm((L, 2, ch, half), bf),
+            vm((2, ch, half), f32), vm((2, L - 1, 2, ch, half), bf), vm((2, L - 1, 2, ch, half), bf),
             vm((ch, half), bf), vm((ch, half), bf), vm((ch, width), f32),
             vm((2, 8, width // 8), f32), vm((8, width // 8), f32), vm((8, width // 8), f32),
             vm((L, 8, width // 8), f32),
             sem((2,)), sem((2,)), sem((2,)), sem((2,)), sem((2,)), sem((2,)), sem((2,)), sem((2,)),
-            sem((L, 2)), sem((L, 2)), sem((1,)), sem((1,)),
-            sem((L,)), sem((L,)), sem((L,)), sem((L,)), sem((2,)), sem((2,)), sem((L,)), sem((L,)),
+            sem((2, L - 1, 2)), sem((2, L - 1, 2)), sem((1,)), sem((1,)),
+            sem((2, L)), sem((2, L)), sem((2, L)), sem((2, L)), sem((2,)), sem((2,)), sem((L,)), sem((L,)),
         ],
         compiler_params=pltpu.CompilerParams(
             collective_id=0, has_side_effects=True, vmem_limit_bytes=58 * 2**20
         ),
-    )(activations, cotangent, wgu, wd, norm_gains[None, :])
+    )(activations, cotangent, jnp.transpose(weights_in, (1, 0, 2)), weights_down, norm_gains[None, :])
     return (
         jnp.stack([g_gate, g_up], axis=1), g_down, g_gains.reshape(width), out.reshape(tok, width),
     )

time: 102 us -> 103 us (level)
  Pallas kernels: 88.2 us -> 92.1 us
  local copies, waits for them, and re-layouts: 9.7 us -> 8.32 us
  other arithmetic: 2.91 us -> 1.76 us
    pallas_call x1, Pallas kernels: 88.2 us -> 92.1 us  [on_device_fused(): pl.pallas_call(functools.partial(fused_kernel, L), out_shape=(shape((hidd...]
    unnamed x11 -> x10, local copies, waits for them, and re-layouts: 5.35 us -> 7.71 us
    pad x1 -> x0, local copies, waits for them, and re-layouts: 2.03 us -> none  [on_device_fused(): wd = jnp.pad(weights_down, pad)]
    slice x1 -> x0, local copies, waits for them, and re-layouts: 1.56 us -> none  [on_device_fused(): weights_in[:, 0]]
    concatenate x1 -> x0, other arithmetic: 1.15 us -> none  [on_device_fused(): jnp.concatenate([jnp.pad(weights_in[:, 0], pad), jnp.pad(weights_in[:, 1]...]
where the time goes in v2:
time: 103 us
  Pallas kernels  92.1 us (89%)
  local copies, waits for them, and re-layouts  8.32 us (8%)
  other arithmetic  1.76 us (2%)
    pallas_call x1, Pallas kernels, on_device_fused(): pl.pallas_call(functools.partial(fused_kernel, L), out_shape=(shape((hidd...  92.1 us
    unnamed x10, local copies, waits for them, and re-layouts  7.71 us

profile of v2, /device:TPU:0, one launch (start us, length us, event | category | flops | bytes accessed | tf_op | source)
XLA Modules:
  0.0 102.9 jit_solution(1546910840278590453)
XLA Ops:
  0.6 2.4 %copy.12 = bf16[108,2,2560]{2,0,1:T(8,128)(2,1)} copy(bf16[108,2,2560]{2,1,0:T(2,128)(2,1)} %param.7) | data formatting | bytes 2211840 | tf_op args[2]
  3.0 92.1 %shard_map.84 = (f32[108,2560]{1,0:T(8,128)}, f32[108,2560]{1,0:T(8,128)}, f32[108,2560]{1,0:T(8,128)}, f32[8,640]{1,0:T(8,128)}, bf16[8,24,5120]{2,1,0:T(8,128)(2,1)}) custom-call(bf16[192,5120]{1,0:T(8,128)(2,1)} %act.1, bf16[192,5120]{1,0:T(8,128)(2,1)} %cot.1, bf16[2,108,2560]{2,1,0:T(8,128)(2,1)} %bitcast.7, bf16[108,2560]{1,0:T(8,128)(2,1)} %w_down.1, ...), custom_call_target="tpu_custom_call" | custom-call | tf_op jit(solution)/shard_map/pallas_call | solution.py:365
  95.1 1.8 %pad_maximum_fusion = f32[108,2,2560]{2,0,1:T(8,128)S(1)} fusion(f32[108,1,2560]{2,0,1:T(8,128)} %bitcast.10, f32[108,1,2560]{2,0,1:T(8,128)} %bitcast.9), kind=kLoop, calls=%fused_computation | loop fusion | flops 552960 | bytes 4423680 | tf_op jit(solution)/shard_map/stack | solution.py:393
  96.9 0.0 copy-start.2
  96.9 0.0 copy-start.1
  96.9 3.1 %copy.10 = f32[108,2,2560]{2,1,0:T(2,128)} copy(f32[108,2,2560]{2,0,1:T(8,128)S(1)} %pad_maximum_fusion) | data formatting | bytes 4423680
  100.0 0.0 copy-done.2
  100.0 0.0 copy-start
  100.0 0.6 reshape.14
  100.6 0.0 copy-done.1
  100.6 1.0 copy.15
  101.6 0.0 copy-done
  101.6 1.3 %copy.16 = bf16[192,5120]{1,0:T(8,128)(2,1)} copy(bf16[192,5120]{1,0:T(8,128)(2,1)S(1)} %bitcast.8) | data formatting | bytes 3932160
Async XLA Ops:
  96.9 3.1 %copy-start.2 = (f32[8,640]{1,0:T(8,128)S(1)}, f32[8,640]{1,0:T(8,128)}, u32[]{:S(2)}) copy-start(f32[8,640]{1,0:T(8,128)} %get-tuple-element.12) | copy-start | bytes 61444
  96.9 3.7 %copy-start.1 = (f32[108,2560]{1,0:T(8,128)S(1)}, f32[108,2560]{1,0:T(8,128)}, u32[]{:S(2)}) copy-start(f32[108,2560]{1,0:T(8,128)} %get-tuple-element.23) | copy-start | bytes 3317764
  100.0 1.6 %copy-start = (bf16[8,24,5120]{2,1,0:T(8,128)(2,1)S(1)}, bf16[8,24,5120]{2,1,0:T(8,128)(2,1)}, u32[]{:S(2)}) copy-start(bf16[8,24,5120]{2,1,0:T(8,128)(2,1)} %get-tuple-element.13) | copy-start | bytes 5898244

commit v3 on v1

--- a/solution.py
+++ b/solution.py
@@ -72,11 +72,11 @@
 
 
 def fused_kernel(
-    L, act, cot, wgu, wd, gains,
+    L, act, cot, w_in, w_down, gains,
     g_gate, g_up, g_down, g_gains, out,
-    normed, xhat, inv_s, cotf, tok_x, part, part_x, dgu, hid,
-    dn, p_buf, r_buf, qf, q_buf, rz, t_buf, t_x, fin, gsum, gx, gc, gz,
-    s_x, r_x, s_c, r_c, s_p, r_p, s_d, r_d, s_z, r_z, s_t, r_t,
+    wgu, wd, normed, xhat, inv_s, cotf, tok_x, part, part_x, dgu, hid,
+    dn, p_buf, r_buf, qf, q_buf, rz, mg, fin, gsum, gx, gc, gz,
+    s_x, r_x, s_c, r_c, s_p, r_p, s_d, r_d, s_z, r_z, r_m,
     s_ag, r_ag, s_fw, r_fw, s_g, r_g, s_gz, r_gz,
 ):
     tok, width = act.shape
@@ -88,7 +88,6 @@
     theirs = pl.ds(pl.multiple_of((1 - d) * half, 128), half)
     x_dev, c_dev = {"dp": 1 - d}, {"fsdp": 1 - f}
     to = [lax.rem(l + k, L) for k in range(L)]
-    frm = [lax.rem(l - k + L, L) for k in range(L)]
 
     def rc(src, dst, ss, rs, dev):
         return pltpu.make_async_remote_copy(
@@ -96,10 +95,18 @@
             device_id=dev, device_id_type=pl.DeviceIdType.MESH,
         )
 
+    peers = [{"loop": to[k]} for k in range(1, L)]
+    peers += [{"loop": to[k], "dp": 1 - d} for k in range(1, L)]
+    inner = jnp.logical_and(l > 0, l < L - 1)
+    outer = jnp.logical_not(inner)
+    via = L - 1 - l
+    far = jnp.where(l == 1, 3, 0)
+    near = 3 - far
+
     barrier = pltpu.get_barrier_semaphore()
-    for dev in [x_dev, c_dev] + [{"loop": to[k]} for k in range(1, L)]:
+    for dev in [x_dev, c_dev] + peers:
         pl.semaphore_signal(barrier, inc=1, device_id=dev, device_id_type=pl.DeviceIdType.MESH)
-    pl.semaphore_wait(barrier, L + 1)
+    pl.semaphore_wait(barrier, 2 * L)
 
     my_rows = pl.ds(pl.multiple_of(f * hb, 16), hb)
     x_cot = rc(cot.at[my_rows, theirs], tok_x.at[1, my_rows], s_x.at[1], r_x.at[1], x_dev)
@@ -122,6 +129,12 @@
     x_nrm = rc(normed.at[my_rows, theirs], tok_x.at[0, my_rows], s_x.at[0], r_x.at[0], x_dev)
     x_nrm.start()
     norm_rows((1 - f) * hb)
+    hidden = w_down.shape[0]
+    low = hidden // 16 * 16
+    for base, dst, src in ((0, wgu, w_in.at[0]), (HP, wgu, w_in.at[1]), (0, wd, w_down)):
+        if low < HP:
+            dst[base + low : base + HP] = jnp.zeros((HP - low, half), jnp.bfloat16)
+        dst[base : base + hidden] = src[...]
 
     part[0, 2] = dot_t(cot[:, mine], wd[...])
     gu = dot_t(normed[:, mine], wgu[...])
@@ -180,50 +193,86 @@
         return copy
 
     p_own.wait()
+    def own(t, j):
+        rows = pl.ds(pl.multiple_of((2 * j + f) * ch, 8), ch)
+        return dn[t, rows, :] + r_buf[t, j].astype(jnp.float32)
+
+    def place(t, j):
+        return {"loop": j, "dp": 1 - d} if t == 1 else {"loop": j}
+
+    def final_send(t, j):
+        return rc(q_buf.at[t, j], rz.at[t, l], s_z.at[t, j], r_z.at[t, l], place(t, j))
+
+    def merge_send(t):
+        return rc(q_buf.at[t, far], mg.at[t], s_z.at[t, far], r_m.at[t], {"loop": via})
+
+    def scatter(t):
+        @pl.when(inner)
+        def _():
+            q_buf[t, far] = own(t, far).astype(jnp.bfloat16)
+            merge_send(t).start()
+
+        for j in (3, 0, 1, 2):
+            go = jnp.logical_or(outer, jnp.logical_and(j != far, j != near))
+            if t == 0:
+                go = jnp.logical_and(go, j != l)
+
+            @pl.when(go)
+            def _():
+                q_buf[t, j] = own(t, j).astype(jnp.bfloat16)
+                final_send(t, j).start()
+
+    def merge(t):
+        @pl.when(inner)
+        def _():
+            merge_send(t).wait_recv()
+            val = own(t, near) + mg[t].astype(jnp.float32)
+            q_buf[t, near] = val.astype(jnp.bfloat16)
+            final_send(t, near).start()
+
     d1 = hidden_grads(1)
+    d1.wait()
+    scatter(1)
     p_oth.wait()
     d0 = hidden_grads(0)
-
-    zc = {}
-    for t, dd in ((1, d1), (0, d0)):
-        dd.wait()
-        for k in (L // 2, *[k for k in range(1, L) if k != L // 2], 0):
-            rows = pl.ds(pl.multiple_of((2 * to[k] + f) * ch, 8), ch)
-            val = dn[t, rows, :] + r_buf[t, to[k]].astype(jnp.float32)
-            if k == 0:
-                qf[t] = val
-            else:
-                q_buf[k, t] = val.astype(jnp.bfloat16)
-                zc[k, t] = rc(q_buf.at[k, t], rz.at[k, t], s_z.at[k, t], r_z.at[k, t], {"loop": to[k]})
-                zc[k, t].start()
+    d0.wait()
+    scatter(0)
 
     def wg_body(i, carry):
         cols = pl.ds(pl.multiple_of(i * 256, 128), 256)
-        own = pl.ds(pl.multiple_of(d * half + i * 256, 128), 256)
-        gu = contract_rows(dgu[0], normed[:, own]) + contract_rows(dgu[1], tok_x[0, :, cols])
-        rows = g_gate.shape[0]
-        g_gate[:, cols] = gu[:rows]
-        g_up[:, cols] = gu[HP : HP + rows]
-        down = contract_rows(hid[0], cot[:, own]) + contract_rows(hid[1], tok_x[1, :, cols])
-        g_down[:, cols] = down[:rows]
+        own_cols = pl.ds(pl.multiple_of(d * half + i * 256, 128), 256)
+        gu = contract_rows(dgu[0], normed[:, own_cols]) + contract_rows(dgu[1], tok_x[0, :, cols])
+        g_gate[:, cols] = gu[:hidden]
+        g_up[:, cols] = gu[HP : HP + hidden]
+        down = contract_rows(hid[0], cot[:, own_cols]) + contract_rows(hid[1], tok_x[1, :, cols])
+        g_down[:, cols] = down[:hidden]
         return carry
 
     lax.fori_loop(0, half // 256, wg_body, 0)
+    merge(1)
+    merge(0)
 
     def total(t):
-        for k in range(1, L):
-            zc[k, t].wait()
-        val = qf[t]
-        for k in range(1, L):
-            val = val + rz[k, t].astype(jnp.float32)
-        return val
-
-    t_buf[...] = total(1).astype(jnp.bfloat16)
-    tc = rc(t_buf, t_x, s_t.at[0], r_t.at[0], x_dev)
-    tc.start()
+        if t == 0:
+            qf[t] = own(t, l)
+        else:
+            qf[t] = jnp.zeros((ch, half), jnp.float32)
+        for p in range(L):
+            got = l != 3 if p == 1 else l != 0 if p == 2 else l >= 0
+            if t == 0:
+                got = jnp.logical_and(got, l != p)
+
+            @pl.when(got)
+            def _():
+                rc(
+                    q_buf.at[t, 0], rz.at[t, p], s_z.at[t, 0], r_z.at[t, p], x_dev
+                ).wait_recv()
+                qf[t] = qf[t] + rz[t, p].astype(jnp.float32)
+
+        return qf[t]
+
+    fin[:, theirs] = total(1)
     fin[:, mine] = total(0)
-    tc.wait()
-    fin[:, theirs] = t_x[...].astype(jnp.float32)
 
     rows = pl.ds(pl.multiple_of((2 * l + f) * ch, 8), ch)
     dnf = fin[...]
@@ -233,12 +282,23 @@
     res = cotf[rows, :] + inv_s[rows, :1] * (scaled - xh * mean)
     slot = 2 * l + f
     out[slot] = res.astype(jnp.bfloat16)
-    ag = {}
-    for k in (L // 2, *[k for k in range(1, L) if k != L // 2]):
-        ag[k] = rc(out.at[slot], out.at[slot], s_ag.at[k], r_ag.at[k], {"loop": to[k]})
-        ag[k].start()
-    fw = {0: rc(out.at[slot], out.at[slot], s_fw.at[0], r_fw.at[0], c_dev)}
-    fw[0].start()
+
+    def chunk(p):
+        return out.at[2 * p + f]
+
+    def hand(p, j, at):
+        return rc(chunk(p), chunk(p), s_ag.at[at], r_ag.at[p], {"loop": j})
+
+    def across(p):
+        return rc(chunk(p), chunk(p), s_fw.at[p], r_fw.at[p], c_dev)
+
+    for j in (1, 2, 0, 3):
+
+        @pl.when(jnp.logical_and(j != l, jnp.logical_or(outer, j != far)))
+        def _():
+            hand(l, j, j).start()
+
+    across(l).start()
 
     gsums = jnp.sum(dnf * xh, axis=0, keepdims=True)
     for i in range(8):
@@ -256,28 +316,40 @@
         gcopies.append(rc(gz.at[l], gz.at[l], s_gz.at[k], r_gz.at[k], {"loop": to[k]}))
         gcopies[-1].start()
 
-    for k in range(1, L):
-        ag[k].wait()
-        got = 2 * frm[k] + f
-        fw[k] = rc(out.at[got], out.at[got], s_fw.at[k], r_fw.at[k], c_dev)
-        fw[k].start()
+    @pl.when(inner)
+    def _():
+        hand(via, near, far).wait_recv()
+        hand(via, near, far).start()
+        across(via).start()
+
+    for p in (1, 2, 0, 3):
+
+        @pl.when(jnp.logical_and(p != l, jnp.logical_or(outer, p != via)))
+        def _():
+            hand(p, near, p).wait_recv()
+            across(p).start()
+
     for copy in gcopies:
         copy.wait()
     acc = gz[0]
     for j in range(1, L):
         acc = acc + gz[j]
     g_gains[...] = acc
-    for k in range(L):
-        fw[k].wait()
+    for p in range(L):
+        across(p).wait()
+
+        @pl.when(p != l)
+        def _():
+            hand(l, p, p).wait_send()
+            final_send(0, p).wait_send()
+
+        final_send(1, p).wait_send()
 
 
 def on_device_fused(L, activations, cotangent, weights_in, weights_down, norm_gains):
     tok, width = activations.shape
     hidden, half = weights_down.shape
     ch = tok // (2 * L)
-    pad = ((0, HP - hidden), (0, 0))
-    wgu = jnp.concatenate([jnp.pad(weights_in[:, 0], pad), jnp.pad(weights_in[:, 1], pad)], axis=0)
-    wd = jnp.pad(weights_down, pad)
     bf, f32 = jnp.bfloat16, jnp.float32
     vm, sem = pltpu.VMEM, pltpu.SemaphoreType.DMA
     spec = pl.BlockSpec(memory_space=pltpu.VMEM)
@@ -291,23 +363,24 @@
         in_specs=[spec] * 5,
         out_specs=(spec,) * 5,
         scratch_shapes=[
+            vm((2 * HP, half), bf), vm((HP, half), bf),
             vm((tok, width), bf), vm((tok, width), f32), vm((tok, 128), f32), vm((tok, width), f32),
             vm((2, tok, half), bf),
             vm((2, 3, tok, HP), f32), vm((4, 3, tok, HP), bf),
             vm((2, tok, 2 * HP), bf), vm((2, tok, HP), bf),
             vm((2, tok, half), f32), vm((2, L, ch, half), bf), vm((2, L, ch, half), bf),
-            vm((2, ch, half), f32), vm((L, 2, ch, half), bf), vm((L, 2, ch, half), bf),
-            vm((ch, half), bf), vm((ch, half), bf), vm((ch, width), f32),
+            vm((2, ch, half), f32), vm((2, L, ch, half), bf), vm((2, L, ch, half), bf),
+            vm((2, ch, half), bf), vm((ch, width), f32),
             vm((2, 8, width // 8), f32), vm((8, width // 8), f32), vm((8, width // 8), f32),
             vm((L, 8, width // 8), f32),
             sem((2,)), sem((2,)), sem((2,)), sem((2,)), sem((2,)), sem((2,)), sem((2,)), sem((2,)),
-            sem((L, 2)), sem((L, 2)), sem((1,)), sem((1,)),
+            sem((2, L)), sem((2, L)), sem((2,)),
             sem((L,)), sem((L,)), sem((L,)), sem((L,)), sem((2,)), sem((2,)), sem((L,)), sem((L,)),
         ],
         compiler_params=pltpu.CompilerParams(
             collective_id=0, has_side_effects=True, vmem_limit_bytes=58 * 2**20
         ),
-    )(activations, cotangent, wgu, wd, norm_gains[None, :])
+    )(activations, cotangent, jnp.transpose(weights_in, (1, 0, 2)), weights_down, norm_gains[None, :])
     return (
         jnp.stack([g_gate, g_up], axis=1), g_down, g_gains.reshape(width), out.reshape(tok, width),
     )
@@ -316,7 +389,7 @@
 def body_for(mesh, args_tok, hidden):
     L = mesh.shape["loop"]
     fits = hidden <= HP and mesh.shape["dp"] == 2 and mesh.shape["fsdp"] == 2 and args_tok % (16 * L) == 0
-    return functools.partial(on_device_fused, L) if fits and L > 1 else on_device
+    return functools.partial(on_device_fused, L) if fits and L == 4 else on_device
 
 
 def solution(mesh):

time: 102 us -> 101 us (level)
  Pallas kernels: 88.2 us -> 89.7 us
  local copies, waits for them, and re-layouts: 9.7 us -> 8.32 us
  other arithmetic: 2.91 us -> 1.76 us
    unnamed x11 -> x10, local copies, waits for them, and re-layouts: 5.35 us -> 7.71 us
    pad x1 -> x0, local copies, waits for them, and re-layouts: 2.03 us -> none  [on_device_fused(): wd = jnp.pad(weights_down, pad)]
    slice x1 -> x0, local copies, waits for them, and re-layouts: 1.56 us -> none  [on_device_fused(): weights_in[:, 0]]
    pallas_call x1, Pallas kernels: 88.2 us -> 89.7 us  [on_device_fused(): pl.pallas_call(functools.partial(fused_kernel, L), out_shape=(shape((hidd...]
    concatenate x1 -> x0, other arithmetic: 1.15 us -> none  [on_device_fused(): jnp.concatenate([jnp.pad(weights_in[:, 0], pad), jnp.pad(weights_in[:, 1]...]
where the time goes in v3:
time: 101 us; the launch traced here: 100 us
  Pallas kernels  89.7 us (89%)
  local copies, waits for them, and re-layouts  8.32 us (8%)
  other arithmetic  1.76 us (2%)
    pallas_call x1, Pallas kernels, on_device_fused(): pl.pallas_call(functools.partial(fused_kernel, L), out_shape=(shape((hidd...  89.7 us
    unnamed x10, local copies, waits for them, and re-layouts  7.71 us

profile of v3, /device:TPU:0, one launch (start us, length us, event | category | flops | bytes accessed | tf_op | source)
XLA Modules:
  0.0 100.4 jit_solution(327923226307137958)
XLA Ops:
  0.6 2.4 %copy.12 = bf16[108,2,2560]{2,0,1:T(8,128)(2,1)} copy(bf16[108,2,2560]{2,1,0:T(2,128)(2,1)} %param.7) | data formatting | bytes 2211840 | tf_op args[2]
  3.0 89.7 %shard_map.84 = (f32[108,2560]{1,0:T(8,128)}, f32[108,2560]{1,0:T(8,128)}, f32[108,2560]{1,0:T(8,128)}, f32[8,640]{1,0:T(8,128)}, bf16[8,24,5120]{2,1,0:T(8,128)(2,1)}) custom-call(bf16[192,5120]{1,0:T(8,128)(2,1)} %act.1, bf16[192,5120]{1,0:T(8,128)(2,1)} %cot.1, bf16[2,108,2560]{2,1,0:T(8,128)(2,1)} %bitcast.7, bf16[108,2560]{1,0:T(8,128)(2,1)} %w_down.1, ...), custom_call_target="tpu_custom_call" | custom-call | tf_op jit(solution)/shard_map/pallas_call | solution.py:357
  92.7 1.8 %pad_maximum_fusion = f32[108,2,2560]{2,0,1:T(8,128)S(1)} fusion(f32[108,1,2560]{2,0,1:T(8,128)} %bitcast.10, f32[108,1,2560]{2,0,1:T(8,128)} %bitcast.9), kind=kLoop, calls=%fused_computation | loop fusion | flops 552960 | bytes 4423680 | tf_op jit(solution)/shard_map/stack | solution.py:385
  94.5 0.0 copy-start.2
  94.5 0.0 copy-start.1
  94.5 3.1 %copy.10 = f32[108,2,2560]{2,1,0:T(2,128)} copy(f32[108,2,2560]{2,0,1:T(8,128)S(1)} %pad_maximum_fusion) | data formatting | bytes 4423680
  97.5 0.0 copy-done.2
  97.5 0.0 copy-start
  97.6 0.6 reshape.14
  98.2 0.0 copy-done.1
  98.2 1.0 copy.15
  99.2 0.0 copy-done
  99.2 1.3 %copy.16 = bf16[192,5120]{1,0:T(8,128)(2,1)} copy(bf16[192,5120]{1,0:T(8,128)(2,1)S(1)} %bitcast.8) | data formatting | bytes 3932160
Async XLA Ops:
  94.5 3.1 %copy-start.2 = (f32[8,640]{1,0:T(8,128)S(1)}, f32[8,640]{1,0:T(8,128)}, u32[]{:S(2)}) copy-start(f32[8,640]{1,0:T(8,128)} %get-tuple-element.12) | copy-start | bytes 61444
  94.5 3.7 %copy-start.1 = (f32[108,2560]{1,0:T(8,128)S(1)}, f32[108,2560]{1,0:T(8,128)}, u32[]{:S(2)}) copy-start(f32[108,2560]{1,0:T(8,128)} %get-tuple-element.23) | copy-start | bytes 3317764
  97.5 1.6 %copy-start = (bf16[8,24,5120]{2,1,0:T(8,128)(2,1)S(1)}, bf16[8,24,5120]{2,1,0:T(8,128)(2,1)}, u32[]{:S(2)}) copy-start(bf16[8,24,5120]{2,1,0:T(8,128)(2,1)} %get-tuple-element.13) | copy-start | bytes 5898244

commit v4 on v3

--- a/solution.py
+++ b/solution.py
@@ -76,12 +76,11 @@
     g_gate, g_up, g_down, g_gains, out,
     wgu, wd, normed, xhat, inv_s, cotf, tok_x, part, part_x, dgu, hid,
     dn, p_buf, r_buf, qf, q_buf, rz, mg, fin, gsum, gx, gc, gz,
-    s_x, r_x, s_c, r_c, s_p, r_p, s_d, r_d, s_z, r_z, r_m,
+    s_x, r_x, s_c, r_c, s_m, r_m2, s_e, r_e, s_p, r_p, s_d, r_d, s_z, r_z, r_m,
     s_ag, r_ag, s_fw, r_fw, s_g, r_g, s_gz, r_gz,
 ):
     tok, width = act.shape
     half = width // 2
-    hb = tok // 2
     ch = tok // (2 * L)
     l, d, f = lax.axis_index("loop"), lax.axis_index("dp"), lax.axis_index("fsdp")
     mine = pl.ds(pl.multiple_of(d * half, 128), half)
@@ -108,9 +107,36 @@
         pl.semaphore_signal(barrier, inc=1, device_id=dev, device_id_type=pl.DeviceIdType.MESH)
     pl.semaphore_wait(barrier, 2 * L)
 
-    my_rows = pl.ds(pl.multiple_of(f * hb, 16), hb)
-    x_cot = rc(cot.at[my_rows, theirs], tok_x.at[1, my_rows], s_x.at[1], r_x.at[1], x_dev)
-    x_cot.start()
+    qt = tok // 4
+    pieces = qt // 16
+    odd = lax.rem(l, 2)
+    mate = l + 1 - 2 * odd
+    first = 2 * odd + f
+    second = 2 * (1 - odd) + f
+
+    def piece(quarter, n):
+        return pl.ds(pl.multiple_of(quarter * qt + n * 16, 16), 16)
+
+    def x_send(a, n):
+        src = cot if a == 1 else normed
+        rows = piece(first, n)
+        return rc(src.at[rows, theirs], tok_x.at[a, rows], s_x.at[a, n], r_x.at[a, n], x_dev)
+
+    def tok_send(a, n, quarter, sems, dev):
+        spot = tok_x.at[a, piece(quarter, n)]
+        return rc(spot, spot, sems[0].at[a, n], sems[1].at[a, n], dev)
+
+    def to_mate(a, n):
+        return tok_send(a, n, first, (s_m, r_m2), {"loop": mate})
+
+    def to_sib(a, n):
+        return tok_send(a, n, first, (s_c, r_c), c_dev)
+
+    def to_sib2(a, n):
+        return tok_send(a, n, second, (s_e, r_e), c_dev)
+
+    for n in range(pieces):
+        x_send(1, n).start()
 
     def norm_rows(start):
         def body(i, carry):
@@ -123,18 +149,27 @@
             normed[rows, :] = (xh * gains[...]).astype(jnp.bfloat16)
             return carry
 
-        lax.fori_loop(0, hb // 16, body, 0)
-
-    norm_rows(f * hb)
-    x_nrm = rc(normed.at[my_rows, theirs], tok_x.at[0, my_rows], s_x.at[0], r_x.at[0], x_dev)
-    x_nrm.start()
-    norm_rows((1 - f) * hb)
+        lax.fori_loop(0, pieces, body, 0)
+
+    norm_rows(first * qt)
+    for n in range(pieces):
+        x_send(0, n).start()
+    for q in range(1, 4):
+        norm_rows(lax.rem(first + q, 4) * qt)
     hidden = w_down.shape[0]
     low = hidden // 16 * 16
     for base, dst, src in ((0, wgu, w_in.at[0]), (HP, wgu, w_in.at[1]), (0, wd, w_down)):
         if low < HP:
             dst[base + low : base + HP] = jnp.zeros((HP - low, half), jnp.bfloat16)
         dst[base : base + hidden] = src[...]
+
+    def forward(a):
+        for n in range(pieces):
+            x_send(a, n).wait_recv()
+            to_mate(a, n).start()
+            to_sib(a, n).start()
+
+    forward(1)
 
     part[0, 2] = dot_t(cot[:, mine], wd[...])
     gu = dot_t(normed[:, mine], wgu[...])
@@ -151,15 +186,18 @@
 
     lax.fori_loop(0, tok // 16, cot_body, 0)
 
-    x_cot.wait()
-    c_cot = rc(tok_x.at[1, my_rows], tok_x.at[1, my_rows], s_c.at[1], r_c.at[1], c_dev)
-    c_cot.start()
-    x_nrm.wait()
-    c_nrm = rc(tok_x.at[0, my_rows], tok_x.at[0, my_rows], s_c.at[0], r_c.at[0], c_dev)
-    c_nrm.start()
-    c_cot.wait()
+    forward(0)
+    for a in (1, 0):
+        for n in range(pieces):
+            to_mate(a, n).wait_recv()
+            to_sib2(a, n).start()
+    for n in range(pieces):
+        to_sib(1, n).wait_recv()
+        to_sib2(1, n).wait_recv()
     part[1, 2] = dot_t(tok_x[1], wd[...])
-    c_nrm.wait()
+    for n in range(pieces):
+        to_sib(0, n).wait_recv()
+        to_sib2(0, n).wait_recv()
     gu = dot_t(tok_x[0], wgu[...])
     part[1, 0] = gu[:, :HP]
     part[1, 1] = gu[:, HP:]
@@ -335,6 +373,12 @@
     for j in range(1, L):
         acc = acc + gz[j]
     g_gains[...] = acc
+    for a in (1, 0):
+        for n in range(pieces):
+            x_send(a, n).wait_send()
+            to_mate(a, n).wait_send()
+            to_sib(a, n).wait_send()
+            to_sib2(a, n).wait_send()
     for p in range(L):
         across(p).wait()
 
@@ -373,7 +417,7 @@
             vm((2, ch, half), bf), vm((ch, width), f32),
             vm((2, 8, width // 8), f32), vm((8, width // 8), f32), vm((8, width // 8), f32),
             vm((L, 8, width // 8), f32),
-            sem((2,)), sem((2,)), sem((2,)), sem((2,)), sem((2,)), sem((2,)), sem((2,)), sem((2,)),
+            *[sem((2, tok // 64))] * 8, sem((2,)), sem((2,)), sem((2,)), sem((2,)),
             sem((2, L)), sem((2, L)), sem((2,)),
             sem((L,)), sem((L,)), sem((L,)), sem((L,)), sem((2,)), sem((2,)), sem((L,)), sem((L,)),
         ],
@@ -388,7 +432,7 @@
 
 def body_for(mesh, args_tok, hidden):
     L = mesh.shape["loop"]
-    fits = hidden <= HP and mesh.shape["dp"] == 2 and mesh.shape["fsdp"] == 2 and args_tok % (16 * L) == 0
+    fits = hidden <= HP and mesh.shape["dp"] == 2 and mesh.shape["fsdp"] == 2 and args_tok % 64 == 0
     return functools.partial(on_device_fused, L) if fits and L == 4 else on_device
 
 

time: 101 us -> 94.8 us (0.939)
  Pallas kernels: 89.7 us -> 83.8 us
    pallas_call x1, Pallas kernels: 89.7 us -> 83.8 us  [on_device_fused(): pl.pallas_call(functools.partial(fused_kernel, L), out_shape=(shape((hidd...]
where the time goes in v4:
time: 94.8 us; the launch traced here: 94.6 us
  Pallas kernels  83.8 us (88%)
  local copies, waits for them, and re-layouts  8.32 us (9%)
  other arithmetic  1.76 us (2%)
    pallas_call x1, Pallas kernels, on_device_fused(): pl.pallas_call(functools.partial(fused_kernel, L), out_shape=(shape((hidd...  83.8 us
    unnamed x10, local copies, waits for them, and re-layouts  7.71 us

profile of v4, /device:TPU:0, one launch (start us, length us, event | category | flops | bytes accessed | tf_op | source)
XLA Modules:
  0.0 94.6 jit_solution(14534762543173240162)
XLA Ops:
  0.6 2.4 %copy.12 = bf16[108,2,2560]{2,0,1:T(8,128)(2,1)} copy(bf16[108,2,2560]{2,1,0:T(2,128)(2,1)} %param.7) | data formatting | bytes 2211840 | tf_op args[2]
  3.0 83.8 %shard_map.84 = (f32[108,2560]{1,0:T(8,128)}, f32[108,2560]{1,0:T(8,128)}, f32[108,2560]{1,0:T(8,128)}, f32[8,640]{1,0:T(8,128)}, bf16[8,24,5120]{2,1,0:T(8,128)(2,1)}) custom-call(bf16[192,5120]{1,0:T(8,128)(2,1)} %act.1, bf16[192,5120]{1,0:T(8,128)(2,1)} %cot.1, bf16[2,108,2560]{2,1,0:T(8,128)(2,1)} %bitcast.7, bf16[108,2560]{1,0:T(8,128)(2,1)} %w_down.1, ...), custom_call_target="tpu_custom_call" | custom-call | tf_op jit(solution)/shard_map/pallas_call | solution.py:401
  86.8 1.8 %pad_maximum_fusion = f32[108,2,2560]{2,0,1:T(8,128)S(1)} fusion(f32[108,1,2560]{2,0,1:T(8,128)} %bitcast.10, f32[108,1,2560]{2,0,1:T(8,128)} %bitcast.9), kind=kLoop, calls=%fused_computation | loop fusion | flops 552960 | bytes 4423680 | tf_op jit(solution)/shard_map/stack | solution.py:429
  88.6 0.0 copy-start.2
  88.6 0.0 copy-start.1
  88.6 3.1 %copy.10 = f32[108,2,2560]{2,1,0:T(2,128)} copy(f32[108,2,2560]{2,0,1:T(8,128)S(1)} %pad_maximum_fusion) | data formatting | bytes 4423680
  91.7 0.0 copy-done.2
  91.7 0.0 copy-start
  91.7 0.6 reshape.14
  92.3 0.0 copy-done.1
  92.3 1.0 %copy.15 = f32[108,2560]{1,0:T(8,128)} copy(f32[108,2560]{1,0:T(8,128)S(1)} %copy-done.1) | data formatting | bytes 2211840
  93.3 0.0 copy-done
  93.3 1.3 %copy.16 = bf16[192,5120]{1,0:T(8,128)(2,1)} copy(bf16[192,5120]{1,0:T(8,128)(2,1)S(1)} %bitcast.8) | data formatting | bytes 3932160
Async XLA Ops:
  88.6 3.1 %copy-start.2 = (f32[8,640]{1,0:T(8,128)S(1)}, f32[8,640]{1,0:T(8,128)}, u32[]{:S(2)}) copy-start(f32[8,640]{1,0:T(8,128)} %get-tuple-element.12) | copy-start | bytes 61444
  88.6 3.7 %copy-start.1 = (f32[108,2560]{1,0:T(8,128)S(1)}, f32[108,2560]{1,0:T(8,128)}, u32[]{:S(2)}) copy-start(f32[108,2560]{1,0:T(8,128)} %get-tuple-element.23) | copy-start | bytes 3317764
  91.7 1.6 %copy-start = (bf16[8,24,5120]{2,1,0:T(8,128)(2,1)S(1)}, bf16[8,24,5120]{2,1,0:T(8,128)(2,1)}, u32[]{:S(2)}) copy-start(bf16[8,24,5120]{2,1,0:T(8,128)(2,1)} %get-tuple-element.13) | copy-start | bytes 5898244

commit v5 on v4

--- a/solution.py
+++ b/solution.py
@@ -73,7 +73,7 @@
 
 def fused_kernel(
     L, act, cot, w_in, w_down, gains,
-    g_gate, g_up, g_down, g_gains, out,
+    g_in, g_down, g_gains, out,
     wgu, wd, normed, xhat, inv_s, cotf, tok_x, part, part_x, dgu, hid,
     dn, p_buf, r_buf, qf, q_buf, rz, mg, fin, gsum, gx, gc, gz,
     s_x, r_x, s_c, r_c, s_m, r_m2, s_e, r_e, s_p, r_p, s_d, r_d, s_z, r_z, r_m,
@@ -280,8 +280,8 @@
         cols = pl.ds(pl.multiple_of(i * 256, 128), 256)
         own_cols = pl.ds(pl.multiple_of(d * half + i * 256, 128), 256)
         gu = contract_rows(dgu[0], normed[:, own_cols]) + contract_rows(dgu[1], tok_x[0, :, cols])
-        g_gate[:, cols] = gu[:hidden]
-        g_up[:, cols] = gu[HP : HP + hidden]
+        g_in[:, 0, cols] = gu[:hidden]
+        g_in[:, 1, cols] = gu[HP : HP + hidden]
         down = contract_rows(hid[0], cot[:, own_cols]) + contract_rows(hid[1], tok_x[1, :, cols])
         g_down[:, cols] = down[:hidden]
         return carry
@@ -398,14 +398,14 @@
     vm, sem = pltpu.VMEM, pltpu.SemaphoreType.DMA
     spec = pl.BlockSpec(memory_space=pltpu.VMEM)
     shape = jax.ShapeDtypeStruct
-    g_gate, g_up, g_down, g_gains, out = pl.pallas_call(
+    g_in, g_down, g_gains, out = pl.pallas_call(
         functools.partial(fused_kernel, L),
         out_shape=(
-            shape((hidden, half), f32), shape((hidden, half), f32), shape((hidden, half), f32),
+            shape((hidden, 2, half), f32), shape((hidden, half), f32),
             shape((8, width // 8), f32), shape((2 * L, ch, width), bf),
         ),
         in_specs=[spec] * 5,
-        out_specs=(spec,) * 5,
+        out_specs=(spec,) * 4,
         scratch_shapes=[
             vm((2 * HP, half), bf), vm((HP, half), bf),
             vm((tok, width), bf), vm((tok, width), f32), vm((tok, 128), f32), vm((tok, width), f32),
@@ -426,7 +426,7 @@
         ),
     )(activations, cotangent, jnp.transpose(weights_in, (1, 0, 2)), weights_down, norm_gains[None, :])
     return (
-        jnp.stack([g_gate, g_up], axis=1), g_down, g_gains.reshape(width), out.reshape(tok, width),
+        g_in, g_down, g_gains.reshape(width), out.reshape(tok, width),
     )
 
 

time: 94.8 us -> 94.9 us (level)
  local copies, waits for them, and re-layouts: 8.32 us -> 10.1 us
  other arithmetic: 1.76 us -> 0 us
    another operation x1 -> x0, other arithmetic: 1.76 us -> none  [on_device_fused(): jnp.stack([g_gate, g_up], axis=1)]
    unnamed x10 -> x8, local copies, waits for them, and re-layouts: 7.71 us -> 8.81 us
where the time goes in v5:
time: 94.9 us; the launch traced here: 94.6 us
  Pallas kernels  83.8 us (88%)
  local copies, waits for them, and re-layouts  10.1 us (11%)
    pallas_call x1, Pallas kernels, on_device_fused(): pl.pallas_call(functools.partial(fused_kernel, L), out_shape=(shape((hidd...  83.8 us
    unnamed x8, local copies, waits for them, and re-layouts  8.81 us

profile of v5, /device:TPU:0, one launch (start us, length us, event | category | flops | bytes accessed | tf_op | source)
XLA Modules:
  0.0 94.6 jit_solution(17009456571850571319)
XLA Ops:
  0.6 2.4 %copy.11 = bf16[108,2,2560]{2,0,1:T(8,128)(2,1)} copy(bf16[108,2,2560]{2,1,0:T(2,128)(2,1)} %param.7) | data formatting | bytes 2211840 | tf_op args[2]
  3.0 83.8 %shard_map.84 = (f32[108,2,2560]{2,1,0:T(2,128)}, f32[108,2560]{1,0:T(8,128)}, f32[8,640]{1,0:T(8,128)}, bf16[8,24,5120]{2,1,0:T(8,128)(2,1)}) custom-call(bf16[192,5120]{1,0:T(8,128)(2,1)} %act.1, bf16[192,5120]{1,0:T(8,128)(2,1)} %cot.1, bf16[2,108,2560]{2,1,0:T(8,128)(2,1)} %bitcast.5, bf16[108,2560]{1,0:T(8,128)(2,1)} %w_down.1, f32[1,5120]{1,0:T(1,128)} %bitcast.7), custom_call_target="tpu_custom_call" | custom-call | tf_op jit(solution)/shard_map/pallas_call | solution.py:401
  86.8 1.3 %reshape.14 = f32[5120]{0:T(1024)} reshape(f32[8,640]{1,0:T(8,128)} %get-tuple-element.10) | data formatting | bytes 40960 | tf_op jit(solution)/shard_map/reshape | solution.py:429
  88.1 0.0 copy-start.1
  88.1 3.2 %copy.15 = f32[108,2,2560]{2,1,0:T(2,128)} copy(f32[108,2,2560]{2,1,0:T(2,128)} %get-tuple-element.16) | data formatting | bytes 4423680
  91.4 0.0 copy-done.1
  91.4 0.0 copy-start
  91.4 1.0 %copy.16 = f32[108,2560]{1,0:T(8,128)} copy(f32[108,2560]{1,0:T(8,128)S(1)} %copy-done.1) | data formatting | bytes 2211840
  92.4 1.0 %copy-done = bf16[8,24,5120]{2,1,0:T(8,128)(2,1)S(1)} copy-done((bf16[8,24,5120]{2,1,0:T(8,128)(2,1)S(1)}, bf16[8,24,5120]{2,1,0:T(8,128)(2,1)}, u32[]{:S(2)}) %copy-start) | copy-done | bytes 1966104
  93.3 1.3 %copy.17 = bf16[192,5120]{1,0:T(8,128)(2,1)} copy(bf16[192,5120]{1,0:T(8,128)(2,1)S(1)} %bitcast.6) | data formatting | bytes 3932160
Async XLA Ops:
  88.1 3.2 %copy-start.1 = (f32[108,2560]{1,0:T(8,128)S(1)}, f32[108,2560]{1,0:T(8,128)}, u32[]{:S(2)}) copy-start(f32[108,2560]{1,0:T(8,128)} %get-tuple-element.17) | copy-start | bytes 3317764
  91.4 2.0 %copy-start = (bf16[8,24,5120]{2,1,0:T(8,128)(2,1)S(1)}, bf16[8,24,5120]{2,1,0:T(8,128)(2,1)}, u32[]{:S(2)}) copy-start(bf16[8,24,5120]{2,1,0:T(8,128)(2,1)} %get-tuple-element.11) | copy-start | bytes 5898244
